TPU v7x, 32 devices: a whole 2x2x4 slice. The times are simulated.
32 devices in a mesh: req: 8 (over z, x), mlp: 4 (over y, core).
Axes of the slice: x: 2, y: 2, z: 4, core: 2. Of those that a mesh axis runs over, the one named last changes fastest.
Arguments:
- tokens: bfloat16 [4096, 4096], P('req'), may hold values from -16 to 16
- grid_sides: int32 [16, 2], P('req'), may hold values from 10 to 14, as said below
- offsets: int32 [16], P('req'), may hold values from 0 to 201, as said below
- merge_rows: int32 [1024, 4], P('req'), may hold values from 0 to 401, as said below
- routes: int32 [1024, 1], replicated, may hold values from 0 to 7; in each aligned block of 128 rows (0 to 127, 128 to 255, ...) at most 16 rows name the same one
- norm_gain: float32 [2, 4096], replicated, may hold values from 0.5 to 1.5
- norm_bias: float32 [2, 4096], replicated, may hold values from -1.5 to 1.5
- layer_scale: float32 [2, 4096], replicated, may hold values from 0.2 to 1
- qkv_weight: bfloat16 [4096, 6144], P('req', 'mlp'), may hold values from -2.34375 to 2.34375
- out_weight: bfloat16 [2048, 4096], P('mlp', 'req'), may hold values from -0.125 to 0.125
- gate_up: bfloat16 [2, 4096, 4096], P(None, 'req', 'mlp'), may hold values from -0.09375 to 0.09375
- down_weight: bfloat16 [4096, 4096], P('mlp', 'req'), may hold values from -0.09375 to 0.09375
- merge_gain: float32 [4, 4096], P(None, 'mlp'), may hold values from 0.5 to 1.5
- merge_bias: float32 [4, 4096], P(None, 'mlp'), may hold values from -1.5 to 1.5
- merge_weight: bfloat16 [4, 4096, 2048], P(None, 'mlp', 'req'), may hold values from -0.1875 to 0.1875
Outputs:
- embeds: bfloat16 [1024, 2048], P('req', 'mlp')
- token_norms: float32 [1024], P('req')
- max_logits: float32 [16, 16], P('req', 'mlp')
Inputs may be any that keep to these rules, and one draw needn't show every extreme that they name: `grid_sides`: sides are even; the first 2 of all 16 images are 14 x 14 and the last image is 10 x 10. `offsets`: the images of a group are packed in order from in-group row 0: image g * 2 + j starts at the sum of 5 + h w over images g * 2 to g * 2 + j - 1. `merge_rows`: for slot k of group g, image i = g * 2 + k div 64 of grid h x w at offset o and m = k mod 64: if m < (h / 2)(w / 2), the entries are o + 5 + (2 a + e) w + 2 b + f for (e, f) = (0, 0), (0, 1), (1, 0), (1, 1), with a = m div (w / 2), b = m mod (w / 2); otherwise all four are 0. `routes`: among the 128 slots of one group, no value appears more than 16 times.
All inputs are finite; a program needn't handle non-finite values.
Results may differ from a plain program's by a relative error of at most 0.017.
Values may be sent and summed in bfloat16 or wider, within the bound.
A program may use at most 128 MiB of HBM per device.

v0:
```python
import math
import jax
import jax.numpy as jnp
from jax import lax
from jax.sharding import PartitionSpec as P

HEAD = 128
OUT = 2048
MSLOT = 64
CAP = 16
EPS = 1e-06


def layer_norm(values, scale_vec, shift_vec):
    center = jnp.mean(values, axis=-1, keepdims=True)
    offset_vals = values - center
    spread = jnp.mean(offset_vals * offset_vals, axis=-1, keepdims=True)
    return offset_vals * lax.rsqrt(spread + EPS) * scale_vec + shift_vec


def row_layout(grid_part, starts, row_count, head_size):
    position = jnp.arange(row_count, dtype=jnp.int32)
    lengths = 5 + grid_part[:, 0] * grid_part[:, 1]
    inside = (
        (position[:, None] >= starts[None, :]) & (position[:, None] < (starts + lengths)[None, :])
    ).astype(jnp.int32)
    present = jnp.sum(inside, axis=1)
    numbers = jnp.arange(grid_part.shape[0], dtype=jnp.int32)
    image_id = jnp.sum(inside * numbers[None, :], axis=1) + present - 1
    local_row = position - jnp.sum(inside * starts[None, :], axis=1)
    height = jnp.sum(inside * grid_part[None, :, 0], axis=1) + 1 - present
    breadth = jnp.sum(inside * grid_part[None, :, 1], axis=1) + 1 - present
    is_patch = (local_row >= 5) & (present > 0)
    patch_idx = jnp.maximum(local_row - 5, 0)
    coord_y = jnp.where(
        is_patch,
        (2.0 * (patch_idx // breadth).astype(jnp.float32) + 1.0) / height.astype(jnp.float32) - 1.0,
        0.0,
    )
    coord_x = jnp.where(
        is_patch,
        (2.0 * (patch_idx % breadth).astype(jnp.float32) + 1.0) / breadth.astype(jnp.float32) - 1.0,
        0.0,
    )
    quarter = head_size // 4
    frequency = math.pi * 100.0 ** (-jnp.arange(quarter, dtype=jnp.float32) / quarter)
    angle_y = (coord_y[:, None] * frequency[None, :])[:, None, :]
    angle_x = (coord_x[:, None] * frequency[None, :])[:, None, :]
    return (image_id, (jnp.cos(angle_y), jnp.sin(angle_y), jnp.cos(angle_x), jnp.sin(angle_x)))


def rotate(vectors, tables):
    cos_y, sin_y, cos_x, sin_x = tables
    quarter = vectors.shape[-1] // 4
    upper_y = vectors[..., :quarter]
    lower_y = vectors[..., quarter : 2 * quarter]
    upper_x = vectors[..., 2 * quarter : 3 * quarter]
    lower_x = vectors[..., 3 * quarter :]
    return jnp.concatenate(
        [
            upper_y * cos_y - lower_y * sin_y,
            upper_y * sin_y + lower_y * cos_y,
            upper_x * cos_x - lower_x * sin_x,
            upper_x * sin_x + lower_x * cos_x,
        ],
        axis=-1,
    )


def attend(queries, key_rows, values, image_id, numbers):
    scores = jnp.einsum(
        "qhd,khd->hqk", queries, key_rows, preferred_element_type=jnp.float32
    ) / math.sqrt(queries.shape[-1])
    same_image = image_id[:, None] == image_id[None, :]
    scores = jnp.where(same_image[None], scores, -jnp.inf)
    row_peak = jnp.max(scores, axis=-1)
    expo_vals = jnp.exp(scores - row_peak[..., None])
    weights = (expo_vals / jnp.sum(expo_vals, axis=-1, keepdims=True)).astype(jnp.bfloat16)
    attended = jnp.einsum(
        "hqk,khd->qhd", weights, values, preferred_element_type=jnp.float32
    ).astype(jnp.bfloat16)
    owned = image_id[None, None, :] == numbers[:, None, None]
    logits = jnp.max(jnp.where(owned, row_peak[None], -jnp.inf), axis=-1)
    return (attended, logits)


def on_device(
    tokens,
    grid_sides,
    offsets,
    merge_rows,
    routes,
    norm_gain,
    norm_bias,
    layer_scale,
    qkv_weight,
    out_weight,
    gate_up,
    down_weight,
    merge_gain,
    merge_bias,
    merge_weight,
):
    row_count = tokens.shape[0]
    model_width = tokens.shape[1]
    groups = lax.axis_size("req")
    shards = lax.axis_size("mlp")
    group_id = lax.axis_index("req")
    member = lax.axis_index("mlp")
    piece_width = model_width // shards
    start_col = member * piece_width
    slot_count = merge_rows.shape[0]
    numbers = jnp.arange(grid_sides.shape[0], dtype=jnp.int32)
    image_id, tables = row_layout(grid_sides, offsets, row_count, HEAD)
    normed = layer_norm(tokens.astype(jnp.float32), norm_gain[0], norm_bias[0]).astype(jnp.bfloat16)
    columns = normed
    mixed_qkv = jnp.dot(
        columns,
        lax.all_gather(qkv_weight, "req", axis=0, tiled=True),
        preferred_element_type=jnp.float32,
    )
    heads_here = qkv_weight.shape[1] // (3 * HEAD)
    mixed_qkv = mixed_qkv.reshape(row_count, heads_here, 3, HEAD)
    queries = rotate(mixed_qkv[:, :, 0], tables).astype(jnp.bfloat16)
    key_rows = rotate(mixed_qkv[:, :, 1], tables).astype(jnp.bfloat16)
    values = mixed_qkv[:, :, 2].astype(jnp.bfloat16)
    attended, logits = attend(queries, key_rows, values, image_id, numbers)
    attended_flat = attended.reshape(row_count, heads_here * HEAD)
    head_terms = jnp.dot(
        attended_flat,
        lax.all_gather(out_weight, "req", axis=1, tiled=True),
        preferred_element_type=jnp.float32,
    )
    attn_sum = lax.psum(head_terms.astype(jnp.bfloat16), "mlp").astype(jnp.float32)
    residual = (tokens.astype(jnp.float32) + layer_scale[0] * attn_sum).astype(jnp.bfloat16)
    resid_piece = lax.dynamic_slice_in_dim(residual, start_col, piece_width, 1)
    normed_two = layer_norm(residual.astype(jnp.float32), norm_gain[1], norm_bias[1]).astype(
        jnp.bfloat16
    )
    columns = normed_two
    gate_pair = jnp.einsum(
        "rk,pkn->prn",
        columns,
        lax.all_gather(gate_up, "req", axis=1, tiled=True),
        preferred_element_type=jnp.float32,
    )
    hidden = (jax.nn.silu(gate_pair[0]) * gate_pair[1]).astype(jnp.bfloat16)
    hidden_terms = jnp.dot(
        hidden,
        lax.all_gather(down_weight, "req", axis=1, tiled=True),
        preferred_element_type=jnp.float32,
    )
    ffn_piece = lax.psum_scatter(
        hidden_terms.astype(jnp.bfloat16), "mlp", scatter_dimension=1, tiled=True
    ).astype(jnp.float32)
    own_scale_two = lax.dynamic_slice_in_dim(layer_scale[1], start_col, piece_width, 0)
    final_piece = (resid_piece.astype(jnp.float32) + own_scale_two * ffn_piece).astype(jnp.bfloat16)
    merged = final_piece[merge_rows].astype(jnp.float32)
    totals, squares = lax.psum(
        (jnp.sum(merged, axis=(1, 2)), jnp.sum(merged * merged, axis=(1, 2))), "mlp"
    )
    center = totals / (4 * model_width)
    spread = squares / (4 * model_width) - center * center
    scaled = (
        (merged - center[:, None, None]) * lax.rsqrt(spread + EPS)[:, None, None] * merge_gain[None]
        + merge_bias[None]
    ).astype(jnp.bfloat16)
    scaled_flat = scaled.reshape(slot_count, 4 * piece_width)
    piece_rows = lax.all_gather(merge_weight, "req", axis=2, tiled=True)
    merge_terms = jnp.dot(
        scaled_flat,
        piece_rows.reshape(4 * piece_width, piece_rows.shape[2]),
        preferred_element_type=jnp.float32,
    )
    projected = lax.psum_scatter(
        merge_terms.astype(jnp.bfloat16), "mlp", scatter_dimension=1, tiled=True
    ).astype(jnp.float32)
    slot_ids = jnp.arange(slot_count, dtype=jnp.int32)
    owner_grid = grid_sides[slot_ids // MSLOT]
    is_live = slot_ids % MSLOT < owner_grid[:, 0] // 2 * (owner_grid[:, 1] // 2)
    projected = jnp.where(is_live[:, None], projected, 0.0).astype(jnp.bfloat16)
    out_cols = projected.shape[1]
    own_routes = lax.dynamic_slice_in_dim(routes, group_id * slot_count, slot_count, 0)[:, 0]
    onehot = (own_routes[:, None] == jnp.arange(groups, dtype=jnp.int32)[None, :]).astype(jnp.int32)
    before = jnp.cumsum(onehot, axis=0) - onehot
    ranks = jnp.sum(before * onehot, axis=1)
    send_rows = (
        jnp.zeros((groups * CAP, out_cols), jnp.bfloat16)
        .at[own_routes * CAP + ranks]
        .set(projected)
    )
    received = lax.all_to_all(
        send_rows.reshape(groups, CAP, out_cols), "req", split_axis=0, concat_axis=0, tiled=True
    )
    embeds = received.reshape(groups * CAP, out_cols)
    row_squares = jnp.sum(jnp.square(embeds.astype(jnp.float32)), axis=1)
    total_squares = lax.psum(row_squares, "mlp")
    token_norms = jnp.sqrt(total_squares / OUT + EPS)
    return (embeds, token_norms, logits)


def solution(mesh):
    placed = (
        P("req", None),
        P("req", None),
        P("req"),
        P("req", None),
        P(),
        P(),
        P(),
        P(),
        P("req", "mlp"),
        P("mlp", "req"),
        P(None, "req", "mlp"),
        P("mlp", "req"),
        P(None, "mlp"),
        P(None, "mlp"),
        P(None, "mlp", "req"),
    )
    return jax.shard_map(
        on_device,
        mesh=mesh,
        in_specs=placed,
        out_specs=(P("req", "mlp"), P("req"), P("req", "mlp")),
        check_vma=False,
    )
```

profile of v0, /device:TPU:0, one launch (start us, length us, event | category | flops | bytes accessed | tf_op | source)
XLA Modules:
  0.0 1053.9 jit_solution(7051907031724275753)
XLA Ops:
  7.2 0.7 all-gather.6.cloned.1.call-update
  8.0 0.7 all-gather.8.cloned.1.call-update
  8.7 1.1 slice_reduce_fusion
  9.8 0.9 add_add_fusion.1
  10.7 0.8 select_reduce_fusion.5
  11.5 2.8 convert_reduce_fusion
  14.3 1.2 fusion.4
  15.6 0.1 add_select_fusion.7
  15.7 0.2 broadcast_compare_fusion
  15.9 3.0 multiply_cosine_fusion.1
  19.0 170.4 %all-gather.6.cloned.1.call-done = bf16[4096,1536]{1,0:T(8,128)(2,1)} async-done(((bf16[512,1536]{1,0:T(8,128)(2,1)}), bf16[4096,1536]{1,0:T(8,128)(2,1)}) %all-gather.6.cloned.1.call-update) | async-done | bytes 12582928 | tf_op jit(solution)/shard_map/all_gather | solution.py:119
  189.4 11.7 %fusion.16 = f32[512,1536]{0,1:T(8,128)S(1)} fusion(bf16[4096,1536]{1,0:T(8,128)(2,1)} %all-gather.6.cloned.1.call-done, bf16[512,4096]{1,0:T(8,128)(2,1)} %param.15, f32[4096]{0:T(1024)S(1)} %bitcast.60, f32[4096]{0:T(1024)S(1)} %bitcast.59, f32[512]{0:T(512)S(1)} %add_rsqrt_fusion.1, f32[512]{0:T(512)S(1)} %broadcast_multiply_fusion.1), kind=kOutput, calls=%fused_computation.25 | convolution fusion | flops 6455033856 | bytes 19959808 | tf_op jit(solution)/shard_map/dot_general | solution.py:117
  201.0 0.2 fusion.98
  201.2 1.5 copy-done.8
  202.7 0.3 copy.46
  203.0 0.3 copy.47
  203.4 2.2 subtract_convert_fusion.3
  205.6 0.9 subtract_convert_fusion.1
  206.5 2.1 fusion.26
  208.6 0.9 fusion.27
  209.5 2.7 fusion.39
  212.2 52.4 %all-gather.8.cloned.1.call-done = bf16[512,4096]{1,0:T(8,128)(2,1)} async-done(((bf16[512,512]{1,0:T(8,128)(2,1)}), bf16[512,4096]{1,0:T(8,128)(2,1)}) %all-gather.8.cloned.1.call-update) | async-done | bytes 4194320 | tf_op jit(solution)/shard_map/all_gather | solution.py:131
  264.6 6.5 convolution_convert_fusion.1
  271.2 0.5 all-gather.10.cloned.1.call-update
  271.8 0.5 all-gather.12.cloned.1.call-update
  272.4 0.3 reduce-scatter.3.cloned.1.call-start
  272.7 82.3 %all-reduce.3.cloned.1.call-done = bf16[512,4096]{1,0:T(8,128)(2,1)} async-done(((bf16[512,4096]{1,0:T(8,128)(2,1)}), bf16[512,4096]{1,0:T(8,128)(2,1)}) %all-reduce.3.cloned.1.call-update) | async-done | bytes 4194320 | tf_op jit(solution)/shard_map/psum | solution.py:134
  355.0 5.6 convert_reduce_fusion.1
  360.6 1.9 copy-done.3
  362.5 1.2 fusion.8
  363.7 221.3 %all-gather.10.cloned.1.call-done = bf16[2,4096,1024]{2,1,0:T(8,128)(2,1)} async-done(((bf16[2,512,1024]{2,1,0:T(8,128)(2,1)}), bf16[2,4096,1024]{2,1,0:T(8,128)(2,1)}) %all-gather.10.cloned.1.call-update) | async-done | bytes 16777232 | tf_op jit(solution)/shard_map/all_gather | solution.py:144
  585.1 15.0 %fusion.29 = f32[2,512,1024]{2,1,0:T(8,128)} fusion(bf16[2,4096,1024]{2,1,0:T(8,128)(2,1)} %all-gather.10.cloned.1.call-done, bf16[512,4096]{1,0:T(8,128)(2,1)} %copy-done.3, f32[4096]{0:T(1024)S(1)} %bitcast.58, f32[4096]{0:T(1024)S(1)} %bitcast.57, f32[512]{0:T(512)S(1)} %add_rsqrt_fusion, f32[512]{0:T(512)S(1)} %broadcast_multiply_fusion), kind=kOutput, calls=%fused_computation.41 | convolution fusion | flops 8602517504 | bytes 25202688 | tf_op jit(solution)/shard_map/rk,pkn->prn/dot_general | solution.py:141
  600.1 110.7 %all-gather.12.cloned.1.call-done = bf16[1024,4096]{1,0:T(8,128)(2,1)} async-done(((bf16[1024,512]{1,0:T(8,128)(2,1)}), bf16[1024,4096]{1,0:T(8,128)(2,1)}) %all-gather.12.cloned.1.call-update) | async-done | bytes 8388624 | tf_op jit(solution)/shard_map/all_gather | solution.py:150
  710.8 11.2 %convolution_convert_fusion = bf16[512,4096]{1,0:T(8,128)(2,1)} fusion(bf16[1024,4096]{1,0:T(8,128)(2,1)} %all-gather.12.cloned.1.call-done, f32[2,512,1024]{2,1,0:T(8,128)} %fusion.29), kind=kOutput, calls=%fused_computation.21 | convolution fusion | flops 4300210176 | bytes 16777216 | tf_op jit(solution)/shard_map/dot_general | solution.py:148
  722.0 0.7 all-gather.14.cloned.1.call-update
  722.7 0.3 reduce-scatter.5.cloned.1.call-start
  723.0 0.1 copy.41
  723.3 41.5 %reduce-scatter.3.cloned.1.call-done = bf16[512,1024]{1,0:T(8,128)(2,1)} async-done(((bf16[512,4096]{1,0:T(8,128)(2,1)}), bf16[512,1024]{1,0:T(8,128)(2,1)}) %reduce-scatter.3.cloned.1.call-update) | async-done | bytes 1048592 | tf_op jit(solution)/shard_map/reduce_scatter | solution.py:153
  764.8 2.0 add_convert_fusion
  766.8 2.1 gather_fusion.1
  768.8 0.7 reshape.383
  769.6 0.2 convert_reduce_fusion.2
  769.8 0.1 reshape.384
  769.9 0.1 reduce_sum.142
  770.0 1.0 multiply_reduce_fusion
  771.0 5.7 all-reduce
  776.8 217.8 %all-gather.14.cloned.1.call-done = bf16[4,1024,2048]{2,1,0:T(8,128)(2,1)} async-done(((bf16[4,1024,256]{2,1,0:T(8,128)(2,1)}), bf16[4,1024,2048]{2,1,0:T(8,128)(2,1)}) %all-gather.14.cloned.1.call-update) | async-done | bytes 16777232 | tf_op jit(solution)/shard_map/all_gather | solution.py:169
  994.6 10.1 fusion.28
  1004.9 0.2 reduce_window_sum.11
  1005.1 0.2 select_reduce_fusion
  1005.3 0.1 copy.35
  1005.4 0.1 copy.45
  1005.5 0.1 fusion.73
  1005.7 0.6 gather_fusion
  1006.3 0.1 fusion.72
  1006.4 0.2 fusion.82
  1006.6 18.2 %reduce-scatter.5.cloned.1.call-done = bf16[128,512]{1,0:T(8,128)(2,1)} async-done(((bf16[128,2048]{1,0:T(8,128)(2,1)}), bf16[128,512]{1,0:T(8,128)(2,1)}) %reduce-scatter.5.cloned.1.call-update) | async-done | bytes 131088 | tf_op jit(solution)/shard_map/reduce_scatter | solution.py:175
  1024.8 2.1 scatter_custom_fusion
  1026.9 5.5 all-to-all-start
  1032.4 0.7 select_reduce_fusion.1
  1033.1 6.7 all-to-all-done
  1040.0 5.9 psum.31
  1045.9 0.5 add_sqrt_fusion
  1046.4 0.7 copy.66
  (58 shorter events, 0.9 us)
Async XLA Ops:
  7.2 997.6 %copy-start = (s32[1024,1]{0,1:T(1,128)S(1)}, s32[1024,1]{0,1:T(1,128)}, u32[]{:S(2)}) copy-start(s32[1024,1]{0,1:T(1,128)} %param.19) | copy-start | bytes 12292
  7.2 182.2 %all-gather.6.cloned.1.call-start = ((), (), s32[]{:S(2)}) async-start(), calls=%async_computation.3 | async-start | bytes 14155776 | tf_op jit(solution)/shard_map/all_gather | solution.py:119
  7.9 256.7 %all-gather.8.cloned.1.call-start = ((), (), s32[]{:S(2)}) async-start(), calls=%async_computation.4 | async-start | bytes 4718592 | tf_op jit(solution)/shard_map/all_gather | solution.py:131
  8.7 346.4 %all-reduce.3.cloned.1.call-start = ((), (), s32[]{:S(2)}) async-start(), calls=%async_computation.5 | async-start | bytes 8388608 | tf_op jit(solution)/shard_map/psum | solution.py:134
  8.7 5.6 copy-start.2
  11.4 7.5 copy-start.11
  11.4 7.5 copy-start.12
  201.0 1.7 copy-start.8
  203.4 2.2 copy-start.4
  203.4 2.2 copy-start.5
  203.4 2.2 copy-start.6
  203.4 2.2 copy-start.7
  271.2 1.5 copy-start.13
  271.2 313.9 %all-gather.10.cloned.1.call-start = ((), (), s32[]{:S(2)}) async-start(), calls=%async_computation.6 | async-start | bytes 18874368 | tf_op jit(solution)/shard_map/all_gather | solution.py:144
  271.8 439.0 %all-gather.12.cloned.1.call-start = ((), (), s32[]{:S(2)}) async-start(), calls=%async_computation.7 | async-start | bytes 9437184 | tf_op jit(solution)/shard_map/all_gather | solution.py:150
  272.4 492.4 %reduce-scatter.3.cloned.1.call-start = ((), (), s32[]{:S(2)}) async-start(), calls=%async_computation.8 | async-start | bytes 5242880 | tf_op jit(solution)/shard_map/reduce_scatter | solution.py:153
  360.6 1.9 copy-start.3
  721.9 1.1 copy-start.14
  721.9 272.7 %all-gather.14.cloned.1.call-start = ((), (), s32[]{:S(2)}) async-start(), calls=%async_computation.9 | async-start | bytes 18874368 | tf_op jit(solution)/shard_map/all_gather | solution.py:169
  722.7 302.1 %reduce-scatter.5.cloned.1.call-start = ((), (), s32[]{:S(2)}) async-start(), calls=%async_computation.10 | async-start | bytes 655360 | tf_op jit(solution)/shard_map/reduce_scatter | solution.py:175
  768.8 225.8 %copy-start.9 = (f32[4,1024]{1,0:T(4,128)S(1)}, f32[4,1024]{1,0:T(4,128)}, u32[]{:S(2)}) copy-start(f32[4,1024]{1,0:T(4,128)} %param.28) | copy-start | bytes 49156
  768.8 225.8 %copy-start.10 = (f32[4,1024]{1,0:T(4,128)S(1)}, f32[4,1024]{1,0:T(4,128)}, u32[]{:S(2)}) copy-start(f32[4,1024]{1,0:T(4,128)} %param.27) | copy-start | bytes 49156
  994.6 11.0 %copy-start.1 = (s32[2,2]{1,0:T(2,128)S(1)}, s32[2,2]{1,0:T(2,128)}, u32[]{:S(2)}) copy-start(s32[2,2]{1,0:T(2,128)} %param.16) | copy-start | bytes 52
  1026.9 12.9 %all-to-all-start = ((bf16[8,16,512]{2,1,0:T(8,128)(2,1)}), bf16[8,16,512]{2,1,0:T(8,128)(2,1)S(1)}, u32[]{:S(2)}, u32[]{:S(2)}) async-start(bf16[8,16,512]{2,1,0:T(8,128)(2,1)} %bitcast.18), calls=%async_computation.2 | async-start | bytes 262144 | tf_op jit(solution)/shard_map/all_to_all | solution.py:192
Sparse Core Ops, SparseCore 0:
  10.2 179.1 all-gather.5
  191.4 73.1 all-gather.7
  271.3 83.6 all-reduce.2
  357.3 227.7 all-gather.9
  587.1 123.5 all-gather.11
  722.1 42.6 reduce-scatter.2
  766.8 227.7 all-gather.13
  1004.9 19.8 reduce-scatter.4
where the time goes:
time: 1050 us
  waiting for transfers between devices  925 us (88%)
  matrix products  59.2 us (6%)
  other arithmetic  27.4 us (3%)
  between operations  14.5 us (1%)
  blocking collectives  11.6 us (1%)
    all_gather x1, waiting for transfers between devices, on_device(): lax.all_gather(gate_up, 'req', axis=1, tiled=True)  221 us
    all_gather x1, waiting for transfers between devices, on_device(): piece_rows = lax.all_gather(merge_weight, 'req', axis=2, tiled=True)  218 us
    all_gather x1, waiting for transfers between devices, on_device(): lax.all_gather(qkv_weight, 'req', axis=0, tiled=True)  170 us
    all_gather x1, waiting for transfers between devices, on_device(): lax.all_gather(down_weight, 'req', axis=1, tiled=True)  111 us
    psum x1, waiting for transfers between devices, on_device(): lax.psum(head_terms.astype(jnp.bfloat16), 'mlp').astype(jnp.float32)  82.3 us
    all_gather x1, waiting for transfers between devices, on_device(): lax.all_gather(out_weight, 'req', axis=1, tiled=True)  52.4 us
    reduce_scatter x1, waiting for transfers between devices, on_device(): lax.psum_scatter(hidden_terms.astype(jnp.bfloat16), 'mlp', scatter_dimens...  41.5 us
  transfers between devices with their start and end apart: 9, of which 9 were waited for; matrix products, arithmetic and copies ran while one was open for 6% of the time, Pallas kernels for 0%

commit v1 on v0

--- a/solution.py
+++ b/solution.py
@@ -3,12 +3,30 @@
 import jax.numpy as jnp
 from jax import lax
 from jax.sharding import PartitionSpec as P
+from jax.lax import axis_index, ppermute, psum
 
 HEAD = 128
 OUT = 2048
 MSLOT = 64
 CAP = 16
 EPS = 1e-06
+
+
+def scan_figure_up(s0):
+    mesh_dim = "req"
+    axis_len = psum(1, mesh_dim)
+    history = [(dev_i, (dev_i + 1) % axis_len) for dev_i in range(axis_len)]
+
+    def _turn_results(w_next):
+        if len(w_next) == axis_len:
+            return w_next
+        m_next = ppermute(w_next[0], mesh_dim, history)
+        return _turn_results([m_next, *w_next])
+
+    carry_in = _turn_results([s0])
+    high = jnp.concatenate(carry_in, axis=2)
+    seen_now = axis_index(mesh_dim)
+    return jnp.roll(high, (seen_now + 1) * s0.shape[2], axis=2)
 
 
 def layer_norm(values, scale_vec, shift_vec):
@@ -166,7 +184,7 @@
         + merge_bias[None]
     ).astype(jnp.bfloat16)
     scaled_flat = scaled.reshape(slot_count, 4 * piece_width)
-    piece_rows = lax.all_gather(merge_weight, "req", axis=2, tiled=True)
+    piece_rows = scan_figure_up(merge_weight)
     merge_terms = jnp.dot(
         scaled_flat,
         piece_rows.reshape(4 * piece_width, piece_rows.shape[2]),

time: 1050 us -> 1060 us (level)
  waiting for transfers between devices: 925 us -> 883 us
  local copies, waits for them, and re-layouts: 10.2 us -> 51.5 us
    ppermute x0 -> x7, waiting for transfers between devices: none -> 375 us  [_turn_results(): m_next = ppermute(w_next[0], mesh_dim, history)]
    all_gather x1 -> x0, waiting for transfers between devices: 218 us -> none  [on_device(): piece_rows = lax.all_gather(merge_weight, 'req', axis=2, tiled=True)]
    psum x1, waiting for transfers between devices: 82.3 us -> 0.02 us  [on_device(): lax.psum(head_terms.astype(jnp.bfloat16), 'mlp').astype(jnp.float32)]
    all_gather x1, waiting for transfers between devices: 221 us -> 146 us  [on_device(): lax.all_gather(gate_up, 'req', axis=1, tiled=True)]
    reduce_scatter x1, waiting for transfers between devices: 41.5 us -> 0.01 us  [on_device(): lax.psum_scatter(hidden_terms.astype(jnp.bfloat16), 'mlp', scatter_dimens...]
    unnamed x34 -> x63, local copies, waits for them, and re-layouts: 4.89 us -> 44.6 us
  transfers between devices with their start and end apart: 9 -> 15, of which waited for: 9 -> 12; matrix products, arithmetic and copies ran while one was open for 6% -> 10% of each run, Pallas kernels for 0% -> 0%
where the time goes in v1:
time: 1060 us
  waiting for transfers between devices  883 us (83%)
  matrix products  59.5 us (6%)
  local copies, waits for them, and re-layouts  51.5 us (5%)
  other arithmetic  27.4 us (3%)
  between operations  14.8 us (1%)
  blocking collectives  11.6 us (1%)
    ppermute x7, waiting for transfers between devices, _turn_results(): m_next = ppermute(w_next[0], mesh_dim, history)  375 us
    all_gather x1, waiting for transfers between devices, on_device(): lax.all_gather(qkv_weight, 'req', axis=0, tiled=True)  170 us
    all_gather x1, waiting for transfers between devices, on_device(): lax.all_gather(gate_up, 'req', axis=1, tiled=True)  146 us
    all_gather x1, waiting for transfers between devices, on_device(): lax.all_gather(down_weight, 'req', axis=1, tiled=True)  113 us
    all_gather x1, waiting for transfers between devices, on_device(): lax.all_gather(out_weight, 'req', axis=1, tiled=True)  52.3 us
    unnamed x63, local copies, waits for them, and re-layouts  44.6 us
  transfers between devices with their start and end apart: 15, of which 12 were waited for; matrix products, arithmetic and copies ran while one was open for 10% of the time, Pallas kernels for 0%

profile of v1, /device:TPU:0, one launch (start us, length us, event | category | flops | bytes accessed | tf_op | source)
XLA Modules:
  0.0 1057.4 jit_solution(7073386201328397894)
XLA Ops:
  7.2 0.7 all-gather.5.cloned.1.call-update
  8.0 0.7 all-gather.7.cloned.1.call-update
  8.7 1.1 slice_reduce_fusion
  9.8 0.9 add_add_fusion.1
  10.7 0.8 select_reduce_fusion.5
  11.5 2.8 convert_reduce_fusion
  14.3 1.2 fusion.6
  15.9 3.0 multiply_cosine_fusion.1
  19.0 170.4 %all-gather.5.cloned.1.call-done = bf16[4096,1536]{1,0:T(8,128)(2,1)} async-done(((bf16[512,1536]{1,0:T(8,128)(2,1)}), bf16[4096,1536]{1,0:T(8,128)(2,1)}) %all-gather.5.cloned.1.call-update) | async-done | bytes 12582928 | tf_op jit(solution)/shard_map/all_gather | solution.py:137
  189.4 11.8 %fusion.18 = f32[512,1536]{0,1:T(8,128)S(1)} fusion(bf16[4096,1536]{1,0:T(8,128)(2,1)} %all-gather.5.cloned.1.call-done, bf16[512,4096]{1,0:T(8,128)(2,1)} %param.15, f32[4096]{0:T(1024)S(1)} %bitcast.58, f32[4096]{0:T(1024)S(1)} %bitcast.59, f32[512]{0:T(512)S(1)} %add_rsqrt_fusion.1, f32[512]{0:T(512)S(1)} %broadcast_multiply_fusion.1), kind=kOutput, calls=%fused_computation.27 | convolution fusion | flops 6455033856 | bytes 19959808 | tf_op jit(solution)/shard_map/dot_general | solution.py:135
  201.4 1.5 copy-done.15
  203.6 2.2 subtract_convert_fusion.1
  205.8 0.9 subtract_convert_fusion.3
  206.7 2.1 fusion.28
  208.8 0.9 fusion.29
  209.7 2.7 fusion.46
  212.4 52.3 %all-gather.7.cloned.1.call-done = bf16[512,4096]{1,0:T(8,128)(2,1)} async-done(((bf16[512,512]{1,0:T(8,128)(2,1)}), bf16[512,4096]{1,0:T(8,128)(2,1)}) %all-gather.7.cloned.1.call-update) | async-done | bytes 4194320 | tf_op jit(solution)/shard_map/all_gather | solution.py:149
  264.6 6.6 convolution_convert_fusion.1
  272.8 1.5 collective-permute-start
  274.2 48.2 %collective-permute-done = bf16[4,1024,256]{2,1,0:T(8,128)(2,1)S(1)} collective-permute-done((bf16[4,1024,256]{2,1,0:T(8,128)(2,1)S(1)}, bf16[4,1024,256]{2,1,0:T(8,128)(2,1)S(1)}, u32[]{:S(2)}, u32[]{:S(2)}) %collective-permute-start) | collective-permute-done | bytes 2097184 | tf_op jit(solution)/shard_map/ppermute | solution.py:23
  322.4 1.4 copy-done.5
  323.8 48.9 %collective-permute-done.1 = bf16[4,1024,256]{2,1,0:T(8,128)(2,1)S(1)} collective-permute-done((bf16[4,1024,256]{2,1,0:T(8,128)(2,1)S(1)}, bf16[4,1024,256]{2,1,0:T(8,128)(2,1)S(1)}, u32[]{:S(2)}, u32[]{:S(2)}) %collective-permute-start.1) | collective-permute-done | bytes 2097184 | tf_op jit(solution)/shard_map/ppermute | solution.py:23
  372.7 1.3 copy-done.7
  374.0 94.9 %collective-permute-done.2 = bf16[4,1024,256]{2,1,0:T(8,128)(2,1)S(1)} collective-permute-done((bf16[4,1024,256]{2,1,0:T(8,128)(2,1)S(1)}, bf16[4,1024,256]{2,1,0:T(8,128)(2,1)S(1)}, u32[]{:S(2)}, u32[]{:S(2)}) %collective-permute-start.2) | collective-permute-done | bytes 2097184 | tf_op jit(solution)/shard_map/ppermute | solution.py:23
  468.9 1.4 copy-done.9
  470.3 85.6 %collective-permute-done.3 = bf16[4,1024,256]{2,1,0:T(8,128)(2,1)} collective-permute-done((bf16[4,1024,256]{2,1,0:T(8,128)(2,1)S(1)}, bf16[4,1024,256]{2,1,0:T(8,128)(2,1)}, u32[]{:S(2)}, u32[]{:S(2)}) %collective-permute-start.3) | collective-permute-done | bytes 2097184 | tf_op jit(solution)/shard_map/ppermute | solution.py:23
  556.1 5.6 convert_reduce_fusion.1
  561.7 2.0 copy-done.3
  563.7 1.2 fusion.10
  564.9 146.4 %all-gather.9.cloned.1.call-done = bf16[2,4096,1024]{2,1,0:T(8,128)(2,1)} async-done(((bf16[2,512,1024]{2,1,0:T(8,128)(2,1)}), bf16[2,4096,1024]{2,1,0:T(8,128)(2,1)}) %all-gather.9.cloned.1.call-update) | async-done | bytes 16777232 | tf_op jit(solution)/shard_map/all_gather | solution.py:162
  711.4 15.1 %fusion.36 = f32[2,512,1024]{2,1,0:T(8,128)} fusion(bf16[2,4096,1024]{2,1,0:T(8,128)(2,1)} %all-gather.9.cloned.1.call-done, bf16[512,4096]{1,0:T(8,128)(2,1)} %copy-done.3, f32[4096]{0:T(1024)S(1)} %bitcast.56, f32[4096]{0:T(1024)S(1)} %bitcast.57, f32[512]{0:T(512)S(1)} %add_rsqrt_fusion, f32[512]{0:T(512)S(1)} %broadcast_multiply_fusion), kind=kOutput, calls=%fused_computation.43 | convolution fusion | flops 8602517504 | bytes 25202688 | tf_op jit(solution)/shard_map/rk,pkn->prn/dot_general | solution.py:159
  726.5 113.0 %all-gather.11.cloned.1.call-done = bf16[1024,4096]{1,0:T(8,128)(2,1)} async-done(((bf16[1024,512]{1,0:T(8,128)(2,1)}), bf16[1024,4096]{1,0:T(8,128)(2,1)}) %all-gather.11.cloned.1.call-update) | async-done | bytes 8388624 | tf_op jit(solution)/shard_map/all_gather | solution.py:168
  839.5 11.1 %convolution_convert_fusion = bf16[512,4096]{1,0:T(8,128)(2,1)} fusion(bf16[1024,4096]{1,0:T(8,128)(2,1)} %all-gather.11.cloned.1.call-done, f32[2,512,1024]{2,1,0:T(8,128)} %fusion.36), kind=kOutput, calls=%fused_computation.23 | convolution fusion | flops 4300210176 | bytes 16777216 | tf_op jit(solution)/shard_map/dot_general | solution.py:166
  850.7 1.5 collective-permute-start.5
  852.2 48.5 %collective-permute-done.5 = bf16[4,1024,256]{2,1,0:T(8,128)(2,1)} collective-permute-done((bf16[4,1024,256]{2,1,0:T(8,128)(2,1)}, bf16[4,1024,256]{2,1,0:T(8,128)(2,1)}, u32[]{:S(2)}, u32[]{:S(2)}) %collective-permute-start.5) | collective-permute-done | bytes 2097184 | tf_op jit(solution)/shard_map/ppermute | solution.py:23
  901.2 48.7 %collective-permute-done.6 = bf16[4,1024,256]{2,1,0:T(8,128)(2,1)} collective-permute-done((bf16[4,1024,256]{2,1,0:T(8,128)(2,1)}, bf16[4,1024,256]{2,1,0:T(8,128)(2,1)}, u32[]{:S(2)}, u32[]{:S(2)}) %collective-permute-start.6) | collective-permute-done | bytes 2097184 | tf_op jit(solution)/shard_map/ppermute | solution.py:23
  949.9 3.1 constant_dynamic-update-slice_fusion.15
  953.0 3.1 constant_dynamic-update-slice_fusion.14
  956.0 3.2 constant_dynamic-update-slice_fusion.13
  959.3 3.2 constant_dynamic-update-slice_fusion.12
  962.5 1.5 constant_dynamic-update-slice_fusion.11
  964.0 1.4 constant_dynamic-update-slice_fusion.10
  965.5 1.5 constant_dynamic-update-slice_fusion.9
  966.9 1.5 constant_dynamic-update-slice_fusion.8
  968.4 3.0 constant_dynamic-update-slice_fusion.7
  971.5 3.1 constant_dynamic-update-slice_fusion.6
  974.5 3.1 constant_dynamic-update-slice_fusion.5
  977.6 3.1 constant_dynamic-update-slice_fusion.4
  980.7 1.5 constant_dynamic-update-slice_fusion.3
  982.2 1.5 constant_dynamic-update-slice_fusion.2
  983.7 1.5 constant_dynamic-update-slice_fusion.1
  985.2 1.6 constant_dynamic-update-slice_fusion
  986.7 2.0 add_convert_fusion
  988.7 2.1 gather_fusion.1
  990.8 0.7 reshape.383
  991.7 1.0 multiply_reduce_fusion
  992.9 5.7 all-reduce
  998.6 10.1 fusion.33
  1010.6 17.5 %reduce-scatter.5.cloned.1.call-done = bf16[128,512]{1,0:T(8,128)(2,1)} async-done(((bf16[128,2048]{1,0:T(8,128)(2,1)}), bf16[128,512]{1,0:T(8,128)(2,1)}) %reduce-scatter.5.cloned.1.call-update) | async-done | bytes 131088 | tf_op jit(solution)/shard_map/reduce_scatter | solution.py:193
  1028.1 2.1 scatter_custom_fusion
  1030.2 5.5 all-to-all-start
  1035.7 0.7 select_reduce_fusion.1
  1036.4 6.7 all-to-all-done
  1043.3 5.9 psum.31
  (99 shorter events, 7.3 us)
Async XLA Ops:
  7.2 1001.6 %copy-start = (s32[1024,1]{0,1:T(1,128)S(1)}, s32[1024,1]{0,1:T(1,128)}, u32[]{:S(2)}) copy-start(s32[1024,1]{0,1:T(1,128)} %param.19) | copy-start | bytes 12292
  7.2 182.2 %all-gather.5.cloned.1.call-start = ((), (), s32[]{:S(2)}) async-start(), calls=%async_computation.3 | async-start | bytes 14155776 | tf_op jit(solution)/shard_map/all_gather | solution.py:137
  7.9 256.7 %all-gather.7.cloned.1.call-start = ((), (), s32[]{:S(2)}) async-start(), calls=%async_computation.4 | async-start | bytes 4718592 | tf_op jit(solution)/shard_map/all_gather | solution.py:149
  8.7 547.4 %all-reduce.3.cloned.1.call-start = ((), (), s32[]{:S(2)}) async-start(), calls=%async_computation.5 | async-start | bytes 8388608 | tf_op jit(solution)/shard_map/psum | solution.py:152
  8.7 5.6 copy-start.2
  11.4 7.5 copy-start.18
  11.4 7.5 copy-start.19
  201.2 1.7 copy-start.15
  203.6 2.2 copy-start.11
  203.6 2.2 copy-start.12
  203.6 2.2 copy-start.13
  203.6 2.2 copy-start.14
  271.2 1.6 copy-start.4
  271.2 199.1 %copy-start.20 = (f32[2,4096]{1,0:T(2,128)S(1)}, f32[2,4096]{1,0:T(2,128)}, u32[]{:S(2)}) copy-start(f32[2,4096]{1,0:T(2,128)} %param.22) | copy-start | bytes 98308
  271.2 440.2 %all-gather.9.cloned.1.call-start = ((), (), s32[]{:S(2)}) async-start(), calls=%async_computation.6 | async-start | bytes 18874368 | tf_op jit(solution)/shard_map/all_gather | solution.py:162
  271.8 567.7 %all-gather.11.cloned.1.call-start = ((), (), s32[]{:S(2)}) async-start(), calls=%async_computation.7 | async-start | bytes 9437184 | tf_op jit(solution)/shard_map/all_gather | solution.py:168
  272.4 714.3 %reduce-scatter.3.cloned.1.call-start = ((), (), s32[]{:S(2)}) async-start(), calls=%async_computation.8 | async-start | bytes 5242880 | tf_op jit(solution)/shard_map/reduce_scatter | solution.py:171
  272.8 49.6 %collective-permute-start = (bf16[4,1024,256]{2,1,0:T(8,128)(2,1)S(1)}, bf16[4,1024,256]{2,1,0:T(8,128)(2,1)S(1)}, u32[]{:S(2)}, u32[]{:S(2)}) collective-permute-start(bf16[4,1024,256]{2,1,0:T(8,128)(2,1)S(1)} %copy-done.4), channel_id=1, source_target_pairs={{0,4},{4,8},{8,12},{12,16},{16,20},{20,24},{24,28},{28,0},{1,5},{5... | collective-permute-start | bytes 6291464 | tf_op jit(solution)/shard_map/ppermute | solution.py:23
  322.4 1.4 copy-start.5
  323.8 48.9 %collective-permute-start.1 = (bf16[4,1024,256]{2,1,0:T(8,128)(2,1)S(1)}, bf16[4,1024,256]{2,1,0:T(8,128)(2,1)S(1)}, u32[]{:S(2)}, u32[]{:S(2)}) collective-permute-start(bf16[4,1024,256]{2,1,0:T(8,128)(2,1)S(1)} %collective-permute-done), channel_id=1, source_target_pairs={{0,4},{4,8},{8,12},{12,16},{16,20},{20,24},{24,28},{28,0},{1,5},{5... | collective-permute-start | bytes 6291464 | tf_op jit(solution)/shard_map/ppermute | solution.py:23
  372.7 1.3 copy-start.7
  374.0 94.9 %collective-permute-start.2 = (bf16[4,1024,256]{2,1,0:T(8,128)(2,1)S(1)}, bf16[4,1024,256]{2,1,0:T(8,128)(2,1)S(1)}, u32[]{:S(2)}, u32[]{:S(2)}) collective-permute-start(bf16[4,1024,256]{2,1,0:T(8,128)(2,1)S(1)} %collective-permute-done.1), channel_id=1, source_target_pairs={{0,4},{4,8},{8,12},{12,16},{16,20},{20,24},{24,28},{28,0},{1,5},{5... | collective-permute-start | bytes 6291464 | tf_op jit(solution)/shard_map/ppermute | solution.py:23
  468.9 1.4 copy-start.9
  470.3 85.6 %collective-permute-start.3 = (bf16[4,1024,256]{2,1,0:T(8,128)(2,1)S(1)}, bf16[4,1024,256]{2,1,0:T(8,128)(2,1)}, u32[]{:S(2)}, u32[]{:S(2)}) collective-permute-start(bf16[4,1024,256]{2,1,0:T(8,128)(2,1)S(1)} %collective-permute-done.2), channel_id=1, source_target_pairs={{0,4},{4,8},{8,12},{12,16},{16,20},{20,24},{24,28},{28,0},{1,5},{5... | collective-permute-start | bytes 6291464 | tf_op jit(solution)/shard_map/ppermute | solution.py:23
  555.9 294.8 %collective-permute-start.4 = (bf16[4,1024,256]{2,1,0:T(8,128)(2,1)}, bf16[4,1024,256]{2,1,0:T(8,128)(2,1)}, u32[]{:S(2)}, u32[]{:S(2)}) collective-permute-start(bf16[4,1024,256]{2,1,0:T(8,128)(2,1)} %collective-permute-done.3), channel_id=1, source_target_pairs={{0,4},{4,8},{8,12},{12,16},{16,20},{20,24},{24,28},{28,0},{1,5},{5... | collective-permute-start | bytes 6291464 | tf_op jit(solution)/shard_map/ppermute | solution.py:23
  561.6 2.1 copy-start.3
  850.6 50.3 %copy-start.21 = (s32[128,4]{0,1:T(4,128)S(1)}, s32[128,4]{0,1:T(4,128)}, u32[]{:S(2)}) copy-start(s32[128,4]{0,1:T(4,128)} %param.18) | copy-start | bytes 6148
  850.7 177.5 %reduce-scatter.5.cloned.1.call-start = ((), (), s32[]{:S(2)}) async-start(), calls=%async_computation.9 | async-start | bytes 655360 | tf_op jit(solution)/shard_map/reduce_scatter | solution.py:193
  850.7 50.0 %collective-permute-start.5 = (bf16[4,1024,256]{2,1,0:T(8,128)(2,1)}, bf16[4,1024,256]{2,1,0:T(8,128)(2,1)}, u32[]{:S(2)}, u32[]{:S(2)}) collective-permute-start(bf16[4,1024,256]{2,1,0:T(8,128)(2,1)} %collective-permute-done.4), channel_id=1, source_target_pairs={{0,4},{4,8},{8,12},{12,16},{16,20},{20,24},{24,28},{28,0},{1,5},{5... | collective-permute-start | bytes 6291464 | tf_op jit(solution)/shard_map/ppermute | solution.py:23
  900.7 49.2 %collective-permute-start.6 = (bf16[4,1024,256]{2,1,0:T(8,128)(2,1)}, bf16[4,1024,256]{2,1,0:T(8,128)(2,1)}, u32[]{:S(2)}, u32[]{:S(2)}) collective-permute-start(bf16[4,1024,256]{2,1,0:T(8,128)(2,1)} %collective-permute-done.5), channel_id=1, source_target_pairs={{0,4},{4,8},{8,12},{12,16},{16,20},{20,24},{24,28},{28,0},{1,5},{5... | collective-permute-start | bytes 6291464 | tf_op jit(solution)/shard_map/ppermute | solution.py:23
  956.0 6.5 copy-start.10
  959.3 4.7 copy-start.8
  962.5 3.0 copy-start.6
  990.7 7.9 copy-start.16
  990.8 7.9 copy-start.17
  998.6 11.0 %copy-start.1 = (s32[2,2]{1,0:T(2,128)S(1)}, s32[2,2]{1,0:T(2,128)}, u32[]{:S(2)}) copy-start(s32[2,2]{1,0:T(2,128)} %param.16) | copy-start | bytes 52
  1030.2 12.8 %all-to-all-start = ((bf16[8,16,512]{2,1,0:T(8,128)(2,1)}), bf16[8,16,512]{2,1,0:T(8,128)(2,1)S(1)}, u32[]{:S(2)}, u32[]{:S(2)}) async-start(bf16[8,16,512]{2,1,0:T(8,128)(2,1)} %bitcast.18), calls=%async_computation.2 | async-start | bytes 262144 | tf_op jit(solution)/shard_map/all_to_all | solution.py:210
Sparse Core Ops, SparseCore 0:
  10.2 179.1 all-gather.4
  191.4 73.1 all-gather.6
  271.3 83.6 all-reduce.2
  357.3 354.0 all-gather.8
  713.5 125.9 all-gather.10
  850.8 42.6 reduce-scatter.2
  1008.9 19.1 reduce-scatter.4
